TPU v7x, 32 devices: a whole 2x2x4 slice. The times are simulated.
32 devices in a mesh: groups: 2 (over x), dp: 16 (over z, y, core).
Axes of the slice: x: 2, y: 2, z: 4, core: 2. Of those that a mesh axis runs over, the one named last changes fastest.
Arguments:
- acts: bfloat16 [5120, 8192], P(('groups', 'dp')), parts along dimension 0, may hold values from -6 to 6
- output_gradient: bfloat16 [5120, 1024], P(('groups', 'dp')), parts along dimension 0, may hold values from -6 to 6
- frozen_weight_codes: bfloat16 [8192, 1024], P('dp'), may hold values from -0.1875 to 0.1875
- weight_block_scale: float32 [64, 8], replicated, may hold values from 0.5 to 2
- adapter_down_weight: bfloat16 [16, 8192, 64], P('dp'), may hold values from -0.75 to 0.75
- adapter_up_weight: bfloat16 [16, 1024, 64], P('dp'), may hold values from -0.1875 to 0.1875
- token_adapter_index: int32 [5120, 1], P('groups'), parts along dimension 0, may hold values from 0 to 15, as said below
- adapter_position: int32 [16], replicated, may hold values from 0 to 15, each once
Outputs:
- input_gradient: bfloat16 [5120, 8192], P(('groups', 'dp')), parts along dimension 0
- down_gradient: float32 [32, 8192, 64], P(('groups', 'dp')), parts along dimension 0
- up_gradient: float32 [32, 1024, 64], P(('groups', 'dp')), parts along dimension 0
There are 2 independent parts, one for each index of `groups`. A program takes and returns all parts, laid end to end along the dimension named above; an argument that names none is the same for every part. Nothing has to cross between parts.
Inputs may be any that keep to these rules, and one draw needn't show every extreme that they name: `token_adapter_index`: all 80 tokens of an aligned unit name one adapter. `adapter_position`: each position once.
All inputs are finite; a program needn't handle non-finite values.
Results may differ from a plain program's by a relative error of at most 0.0051.
Values may be sent and summed in bfloat16 or wider, within the bound.
A program may use at most 192 MiB of HBM per device.

v0:
```python
import functools

import jax
import jax.numpy as jnp
from jax import lax
from jax.experimental import pallas as pl
from jax.experimental.pallas import tpu as pltpu
from jax.sharding import PartitionSpec as P

BLK = 128
SLOTS = 2
NT = (((1,), (1,)), ((), ()))
TN = (((0,), (0,)), ((), ()))
F32 = jnp.float32
BF16 = jnp.bfloat16


def slab_kernel(unit_rows, place, grads, acts, weight, up, down, out, proj, summed):
    step = pl.program_id(0)

    @pl.when(step == 0)
    def _():
        summed[...] = jnp.zeros_like(summed)

    base = lax.dot_general(grads[...], weight[...], NT, preferred_element_type=F32)
    units = grads.shape[0] // unit_rows
    for u in range(units):
        rows = pl.ds(u * unit_rows, unit_rows)
        p = place[step * units + u]
        down_p = down[p]
        x = acts[rows, :]
        low = lax.dot_general(grads[rows, :], up[p], NT, preferred_element_type=F32).astype(BF16)
        proj[rows, :] = lax.dot_general(x, down_p, NT, preferred_element_type=F32)
        back = (0.5 * jnp.dot(low, down_p, preferred_element_type=F32)).astype(BF16)
        here = base[u * unit_rows : (u + 1) * unit_rows, :]
        out[rows, :] = (here + back.astype(F32)).astype(BF16)
        summed[p] += 0.5 * lax.dot_general(low, x, TN, preferred_element_type=F32)


def up_kernel(place_ref, me_ref, grads, proj, total):
    step = pl.program_id(0)
    unit_rows = grads.shape[0]

    @pl.when(step == 0)
    def _():
        total[...] = jnp.zeros_like(total)

    @pl.when(place_ref[step] == me_ref[0])
    def _():
        total[...] += 0.5 * lax.dot_general(
            proj[...], grads[...], TN, preferred_element_type=F32
        )


def shards(
    acts,
    output_gradient,
    frozen_weight_codes,
    weight_block_scale,
    adapter_down_weight,
    adapter_up_weight,
    token_adapter_index,
    adapter_position,
):
    token_rows, row_extent = acts.shape
    out_width = output_gradient.shape[1]
    rank = adapter_down_weight.shape[2]
    n = lax.axis_size("dp")
    me = lax.axis_index("dp")
    unit_rows = token_rows // SLOTS
    slab = row_extent // n
    tokens = token_rows * n
    unit_place = adapter_position[token_adapter_index[::unit_rows, 0]]

    grads_all = lax.all_gather(output_gradient, "dp", axis=0, tiled=True)
    up_all = lax.all_gather(adapter_up_weight.transpose(0, 2, 1), "dp", axis=0, tiled=True)
    down_slabs = lax.all_to_all(
        adapter_down_weight.transpose(0, 2, 1), "dp", split_axis=2, concat_axis=0, tiled=True
    )
    acts_slab = lax.all_to_all(acts, "dp", split_axis=1, concat_axis=0, tiled=True)

    row_ids = me * slab + jnp.arange(slab, dtype=jnp.int32)
    scale_rows = weight_block_scale[row_ids // BLK]
    codes = frozen_weight_codes.astype(F32).reshape(slab, out_width // BLK, BLK)
    weight = (codes * scale_rows[:, :, None]).astype(BF16).reshape(slab, out_width)

    adapters = up_all.shape[0]
    rows = 2 * token_rows
    whole = lambda *shape: pl.BlockSpec(shape, lambda i, place: (0,) * len(shape))
    out, proj_part, summed = pl.pallas_call(
        functools.partial(slab_kernel, unit_rows),
        grid_spec=pltpu.PrefetchScalarGridSpec(
            num_scalar_prefetch=1,
            grid=(tokens // rows,),
            in_specs=[
                pl.BlockSpec((rows, out_width), lambda i, place: (i, 0)),
                pl.BlockSpec((rows, slab), lambda i, place: (i, 0)),
                whole(slab, out_width),
                whole(adapters, rank, out_width),
                whole(adapters, rank, slab),
            ],
            out_specs=[
                pl.BlockSpec((rows, slab), lambda i, place: (i, 0)),
                pl.BlockSpec((rows, rank), lambda i, place: (i, 0)),
                whole(adapters, rank, slab),
            ],
        ),
        out_shape=[
            jax.ShapeDtypeStruct((tokens, slab), BF16),
            jax.ShapeDtypeStruct((tokens, rank), F32),
            jax.ShapeDtypeStruct((adapters, rank, slab), F32),
        ],
        compiler_params=pltpu.CompilerParams(vmem_limit_bytes=56 * 2**20),
    )(unit_place, grads_all, acts_slab, weight, up_all, down_slabs)

    proj_own = lax.psum_scatter(proj_part, "dp", scatter_dimension=0, tiled=True).astype(BF16)
    proj_all = lax.all_gather(proj_own, "dp", axis=0, tiled=True)
    input_gradient = lax.all_to_all(out, "dp", split_axis=0, concat_axis=1, tiled=True)
    down_gradient = lax.all_to_all(
        summed.astype(BF16), "dp", split_axis=0, concat_axis=2, tiled=True
    ).astype(F32)
    up_gradient = pl.pallas_call(
        up_kernel,
        grid_spec=pltpu.PrefetchScalarGridSpec(
            num_scalar_prefetch=2,
            grid=(tokens // unit_rows,),
            in_specs=[
                pl.BlockSpec((unit_rows, out_width), lambda i, place, me: (i, 0)),
                pl.BlockSpec((unit_rows, rank), lambda i, place, me: (i, 0)),
            ],
            out_specs=pl.BlockSpec((rank, out_width), lambda i, place, me: (0, 0)),
        ),
        out_shape=jax.ShapeDtypeStruct((rank, out_width), F32),
    )(unit_place, me.astype(jnp.int32).reshape(1), grads_all, proj_all)
    return (
        input_gradient,
        down_gradient.transpose(0, 2, 1),
        up_gradient[None].transpose(0, 2, 1),
    )


def solution(mesh):
    placed = (
        P(("groups", "dp"), None),
        P(("groups", "dp"), None),
        P("dp", None),
        P(),
        P("dp", None, None),
        P("dp", None, None),
        P("groups", None),
        P(),
    )
    return jax.shard_map(
        shards,
        mesh=mesh,
        in_specs=placed,
        out_specs=(
            P(("groups", "dp"), None),
            P(("groups", "dp"), None, None),
            P(("groups", "dp"), None, None),
        ),
        check_vma=False,
    )
```

profile of v0, /device:TPU:0, one launch (start us, length us, event | category | flops | bytes accessed | tf_op | source)
XLA Modules:
  0.0 373.8 jit_solution(11794910068177935209)
XLA Ops:
  7.2 0.0 copy-start
  7.2 0.0 all-gather.6.cloned.1.call-start
  7.2 0.7 all-gather.6.cloned.1.call-update
  7.9 0.0 all-gather.4.cloned.1.call-start
  8.0 0.7 all-gather.4.cloned.1.call-update
  8.7 9.2 %copy.21 = bf16[1,8192,64]{2,0,1:T(2,128)(2,1)} copy(bf16[1,8192,64]{1,2,0:T(8,128)(2,1)} %param.12) | data formatting | bytes 2097152 | tf_op args[4]
  17.9 8.5 %bitcast_bitcast_fusion = bf16[8192,1,64]{2,1,0:T(2,128)(2,1)} fusion(bf16[1,8192,64]{2,0,1:T(2,128)(2,1)} %copy.21), kind=kLoop, calls=%fused_computation.16 | loop fusion | bytes 2097152
  26.4 0.5 broadcast.85
  26.9 45.2 %reduce = bf16[8192,64]{1,0:T(8,128)(2,1)S(1)} reduce(bf16[8192,1,64]{2,1,0:T(2,128)(2,1)} %bitcast_bitcast_fusion, bf16[]{:T(256)} %broadcast.85), dimensions={1}, to_apply=%bitcast_bitcast_fusion.reduce_sub_computation | reduce | bytes 2097154
  72.1 2.3 reshape.118
  74.4 7.4 %all-to-all-start.1 = ((bf16[16,2,16384]{2,1,0:T(2,128)(2,1)}), bf16[16,2,16384]{2,1,0:T(2,128)(2,1)S(1)}, u32[]{:S(2)}, u32[]{:S(2)}) async-start(bf16[16,2,16384]{2,1,0:T(2,128)(2,1)} %reshape.118), calls=%async_computation.1 | async-start | bytes 2097152 | tf_op jit(solution)/shard_map/all_to_all | solution.py:77
  81.8 3.6 copy.37
  85.4 36.0 %all-to-all-done.1 = bf16[16,2,16384]{2,1,0:T(2,128)(2,1)S(1)} async-done(((bf16[16,2,16384]{2,1,0:T(2,128)(2,1)}), bf16[16,2,16384]{2,1,0:T(2,128)(2,1)S(1)}, u32[]{:S(2)}, u32[]{:S(2)}) %all-to-all-start.1) | async-done | bytes 1048608 | tf_op jit(solution)/shard_map/all_to_all | solution.py:77
  121.4 0.0 copy-start.2
  121.4 0.0 copy-start.4
  121.4 1.0 copy-done.2
  122.4 11.4 %all-to-all-start = ((bf16[160,16,512]{2,0,1:T(8,128)(2,1)}), bf16[160,16,512]{2,0,1:T(8,128)(2,1)S(1)}, u32[]{:S(2)}, u32[]{:S(2)}) async-start(bf16[160,16,512]{2,0,1:T(8,128)(2,1)} %bitcast.44), calls=%async_computation | async-start | bytes 5242880 | tf_op jit(solution)/shard_map/all_to_all | solution.py:80
  133.8 0.8 slice.3
  134.6 0.0 copy-done.4
  134.6 0.1 copy.20
  134.7 0.0 copy-done
  134.7 1.2 gather_fusion
  136.0 1.0 gather_fusion.1
  137.0 0.0 copy-start.3
  137.0 0.6 mul.15
  137.6 0.6 copy-done.3
  138.2 1.6 fusion.weight
  139.8 10.2 %reshape.119 = bf16[8192,1,64]{2,1,0:T(2,128)(2,1)} reshape(bf16[16,2,16384]{2,1,0:T(2,128)(2,1)} %copy-done.2) | data formatting | bytes 2097152
  150.0 3.8 %copy.30 = bf16[1,64,8192]{1,2,0:T(8,128)(2,1)} copy(bf16[1,64,8192]{1,0,2:T(2,128)(2,1)} %bitcast.45) | data formatting | bytes 2097152
  153.8 2.7 copy.23
  156.5 0.0 all-gather.6.cloned.1.call-done.up
  156.5 27.5 %all-to-all-done = bf16[160,16,512]{2,0,1:T(8,128)(2,1)S(1)} async-done(((bf16[160,16,512]{2,0,1:T(8,128)(2,1)}), bf16[160,16,512]{2,0,1:T(8,128)(2,1)S(1)}, u32[]{:S(2)}, u32[]{:S(2)}) %all-to-all-start) | async-done | bytes 2621472 | tf_op jit(solution)/shard_map/all_to_all | solution.py:80
  184.0 0.0 copy-start.1
  184.0 0.0 all-gather.4.cloned.1.call-done.grads
  184.0 1.5 copy-done.1
  185.5 17.8 %shard_map.103 = (bf16[2560,512]{1,0:T(8,128)(2,1)}, f32[2560,64]{1,0:T(8,128)}, f32[16,64,512]{2,1,0:T(8,128)}) custom-call(s32[32]{0:T(128)} %gather_fusion, bf16[2560,1024]{1,0:T(8,128)(2,1)} %all-gather.4.cloned.1.call-done.grads, bf16[2560,512]{1,0:T(8,128)(2,1)} %bitcast.47, bf16[512,1024]{1,0:T(8,128)(2,1)} %fusion.weight, ...), custom_call_target="tpu_custom_call" | custom-call | tf_op jit(solution)/shard_map/pallas_call | solution.py:90
  203.3 1.7 convert_element_type.33
  205.0 38.1 %all_to_all.65 = bf16[16,64,512]{2,1,0:T(8,128)(2,1)} all-to-all(bf16[16,64,512]{2,1,0:T(8,128)(2,1)S(1)} %convert_element_type.33), channel_id=1, replica_groups=mesh['groups'=2,'dp'=16] {'dp'}, dimensions={0} | all-to-all | bytes 2097152 | tf_op jit(solution)/shard_map/all_to_all | solution.py:119
  243.1 5.0 %all-to-all-start.2 = ((bf16[16,160,512]{2,1,0:T(8,128)(2,1)}), bf16[16,160,512]{2,1,0:T(8,128)(2,1)S(1)}, u32[]{:S(2)}, u32[]{:S(2)}) async-start(bf16[16,160,512]{2,1,0:T(8,128)(2,1)} %bitcast.53), calls=%async_computation.2 | async-start | bytes 5242880 | tf_op jit(solution)/shard_map/all_to_all | solution.py:118
  248.1 0.0 reduce-scatter.2.cloned.1.call-start
  248.1 0.7 reduce-scatter.2.cloned.1.call-update
  248.8 73.3 %reduce-scatter.2.cloned.1.call-done = f32[160,64]{1,0:T(8,128)} async-done(((f32[2560,64]{1,0:T(8,128)}), f32[160,64]{1,0:T(8,128)}) %reduce-scatter.2.cloned.1.call-update) | async-done | bytes 40976 | tf_op jit(solution)/shard_map/reduce_scatter | solution.py:116
  322.2 0.9 convert_bitcast_fusion.1
  323.1 0.1 copy.26
  323.2 20.9 %all-gather = bf16[16,160,64]{1,2,0:T(8,128)(2,1)S(1)} all-gather(bf16[1,160,64]{1,2,0:T(8,128)(2,1)S(1)} %copy.26), channel_id=1, replica_groups=mesh['groups'=2,'dp'=16] {'dp'}, dimensions={0}, use_global_device_ids=true | all-gather | bytes 348160 | tf_op jit(solution)/shard_map/all_gather | solution.py:117
  344.1 1.1 copy.27
  345.2 17.3 %shard_map.104 = f32[64,1024]{1,0:T(8,128)} custom-call(s32[32]{0:T(128)} %gather_fusion, s32[1]{0:T(128)} %bitcast.13.me_ref, bf16[2560,1024]{1,0:T(8,128)(2,1)} %all-gather.4.cloned.1.call-done.grads, bf16[2560,64]{1,0:T(8,128)(2,1)} %bitcast.51), custom_call_target="tpu_custom_call" | custom-call | tf_op jit(solution)/shard_map/pallas_call | solution.py:122
  362.5 1.5 convert_bitcast_fusion
  364.0 1.5 copy.33
  365.5 0.0 all-to-all-done.2
  365.5 1.8 copy.32
  (4 shorter events, 0.0 us)
Async XLA Ops:
  7.2 127.5 %copy-start = (s32[16]{0:T(128)S(1)}, s32[16]{0:T(128)}, u32[]{:S(2)}) copy-start(s32[16]{0:T(128)} %param.15) | copy-start | bytes 196
  7.2 149.3 %all-gather.6.cloned.1.call-start = ((), (), s32[]{:S(2)}) async-start(), calls=%async_computation.6 | async-start | bytes 2228224 | tf_op jit(solution)/shard_map/all_gather | solution.py:76
  7.9 176.1 %all-gather.4.cloned.1.call-start = ((), (), s32[]{:S(2)}) async-start(), calls=%async_computation.5 | async-start | bytes 5570560 | tf_op jit(solution)/shard_map/all_gather | solution.py:75
  74.4 47.0 %all-to-all-start.1 = ((bf16[16,2,16384]{2,1,0:T(2,128)(2,1)}), bf16[16,2,16384]{2,1,0:T(2,128)(2,1)S(1)}, u32[]{:S(2)}, u32[]{:S(2)}) async-start(bf16[16,2,16384]{2,1,0:T(2,128)(2,1)} %reshape.118), calls=%async_computation.1 | async-start | bytes 2097152 | tf_op jit(solution)/shard_map/all_to_all | solution.py:77
  121.4 1.0 copy-start.2
  121.4 13.2 %copy-start.4 = (f32[64,8]{0,1:T(8,128)S(1)}, f32[64,8]{0,1:T(8,128)}, u32[]{:S(2)}) copy-start(f32[64,8]{0,1:T(8,128)} %param.11) | copy-start | bytes 6148
  122.4 61.6 %all-to-all-start = ((bf16[160,16,512]{2,0,1:T(8,128)(2,1)}), bf16[160,16,512]{2,0,1:T(8,128)(2,1)S(1)}, u32[]{:S(2)}, u32[]{:S(2)}) async-start(bf16[160,16,512]{2,0,1:T(8,128)(2,1)} %bitcast.44), calls=%async_computation | async-start | bytes 5242880 | tf_op jit(solution)/shard_map/all_to_all | solution.py:80
  137.0 1.2 copy-start.3
  184.0 1.5 copy-start.1
  243.1 122.4 %all-to-all-start.2 = ((bf16[16,160,512]{2,1,0:T(8,128)(2,1)}), bf16[16,160,512]{2,1,0:T(8,128)(2,1)S(1)}, u32[]{:S(2)}, u32[]{:S(2)}) async-start(bf16[16,160,512]{2,1,0:T(8,128)(2,1)} %bitcast.53), calls=%async_computation.2 | async-start | bytes 5242880 | tf_op jit(solution)/shard_map/all_to_all | solution.py:118
  248.1 74.1 %reduce-scatter.2.cloned.1.call-start = ((), (), s32[]{:S(2)}) async-start(), calls=%async_computation.7 | async-start | bytes 1392640 | tf_op jit(solution)/shard_map/reduce_scatter | solution.py:116
Sparse Core Ops, SparseCore 0:
  10.2 44.0 all-gather.5
  56.6 74.1 all-gather.3
  252.6 69.5 reduce-scatter.1
where the time goes:
time: 376 us; the launch traced here: 374 us
  waiting for transfers between devices  139 us (37%)
  blocking collectives  59 us (16%)
  local copies, waits for them, and re-layouts  52.2 us (14%)
  other arithmetic  50.9 us (14%)
  Pallas kernels  35.1 us (9%)
  starting transfers between devices  23.9 us (6%)
  between operations  13.9 us (4%)
    reduce_scatter x1, waiting for transfers between devices, shards(): lax.psum_scatter(proj_part, 'dp', scatter_dimension=0, tiled=True)  73.3 us
    unnamed x3, other arithmetic  47.6 us
    all_to_all x1, blocking collectives, shards(): lax.all_to_all(summed.astype(BF16), 'dp', split_axis=0, concat_axis=2, ti...  38.1 us
    unnamed x18, local copies, waits for them, and re-layouts  37.7 us
    all_to_all x1, waiting for transfers between devices, shards(): lax.all_to_all(adapter_down_weight.transpose(0, 2, 1), 'dp', split_axis=2...  36 us
    all_to_all x1, waiting for transfers between devices, shards(): lax.all_to_all(acts, 'dp', split_axis=1, concat_axis=0, tiled=True)  27.5 us
    all_gather x1, blocking collectives, shards(): proj_all = lax.all_gather(proj_own, 'dp', axis=0, tiled=True)  20.9 us
    pallas_call x1, Pallas kernels, shards(): pl.pallas_call(functools.partial(slab_kernel, unit_rows), grid_spec=pltpu...  17.8 us
  transfers between devices with their start and end apart: 6, of which 3 were waited for; matrix products, arithmetic and copies ran while one was open for 26% of the time, Pallas kernels for 5%

commit v1 on v0

--- a/solution.py
+++ b/solution.py
@@ -50,6 +50,190 @@
         total[...] += 0.5 * lax.dot_general(
             proj[...], grads[...], TN, preferred_element_type=F32
         )
+
+
+def fused_kernel(n, unit_rows, place, acts, grads, weight, up, down, out, dgrad, ugrad,
+                 part, part_in, own, projs, stage, landed, spread, dsend, dland,
+                 part_s, part_r, proj_s, proj_r, out_s, out_r, down_s, down_r):
+    me = lax.axis_index("dp")
+    rows = SLOTS * unit_rows
+    slab = weight.shape[0]
+    rank = down.shape[1]
+    wide = SLOTS * rank
+
+    def peer(s):
+        return lax.rem(me + s, n)
+
+    def send(src, dst, send_sem, recv_sem, j):
+        return pltpu.make_async_remote_copy(
+            src_ref=src, dst_ref=dst, send_sem=send_sem.at[j], recv_sem=recv_sem.at[me],
+            device_id={"dp": j}, device_id_type=pl.DeviceIdType.MESH)
+
+    def arrival(src, dst, send_sem, recv_sem, j):
+        return pltpu.make_async_remote_copy(
+            src_ref=src, dst_ref=dst, send_sem=send_sem.at[j], recv_sem=recv_sem.at[j],
+            device_id={"dp": j}, device_id_type=pl.DeviceIdType.MESH)
+
+    barrier = pltpu.get_barrier_semaphore()
+
+    @pl.loop(1, n)
+    def _(s):
+        pl.semaphore_signal(barrier, inc=1, device_id={"dp": peer(s)},
+                            device_id_type=pl.DeviceIdType.MESH)
+
+    pl.semaphore_wait(barrier, n - 1)
+
+    def tile(j, u):
+        return pl.ds(pl.multiple_of(j * rows + u * unit_rows, 16), unit_rows)
+
+    def project(j, dst):
+        both = [
+            lax.dot_general(acts[tile(j, u), :], down[place[SLOTS * j + u]], NT,
+                            preferred_element_type=F32)
+            for u in range(SLOTS)
+        ]
+        dst[j] = jnp.concatenate(both, axis=1)
+
+    @pl.loop(1, n)
+    def _(s):
+        j = peer(s)
+        project(j, part)
+        send(part.at[j], part_in.at[me], part_s, part_r, j).start()
+
+    project(me, part_in)
+
+    lane_half = lax.broadcasted_iota(jnp.int32, (unit_rows, 2 * rank), 1) // rank
+
+    def block(j, dst):
+        for u in range(SLOTS):
+            at = tile(j, u)
+            p = place[SLOTS * j + u]
+            g = grads[at, :]
+            low = lax.dot_general(g, up[p], NT, preferred_element_type=F32).astype(BF16)
+            base = lax.dot_general(g, weight[...], NT, preferred_element_type=F32)
+            back = (0.5 * jnp.dot(low, down[p], preferred_element_type=F32)).astype(BF16)
+            dst[j, pl.ds(u * unit_rows, unit_rows), :] = (base + back.astype(F32)).astype(BF16)
+            low = low.astype(F32)
+            twice = jnp.concatenate([low, low], axis=1)
+            for c in range(n // 2):
+                kept = jnp.where(lane_half + 2 * c == p, twice, 0.0)
+                spread[at, pl.ds(c * 2 * rank, 2 * rank)] = kept.astype(BF16)
+
+    @pl.loop(1, n)
+    def _(s):
+        j = peer(s)
+        block(j, stage)
+        send(stage.at[j], landed.at[me], out_s, out_r, j).start()
+
+    block(me, landed)
+
+    @pl.loop(1, n)
+    def _(s):
+        j = peer(s)
+        arrival(part.at[j], part_in.at[j], part_s, part_r, j).wait()
+
+    total = part_in[0]
+    for j in range(1, n):
+        total = total + part_in[j]
+    own[...] = total.astype(BF16)
+
+    @pl.loop(1, n)
+    def _(s):
+        j = peer(s)
+        send(own, projs.at[me], proj_s, proj_r, j).start()
+
+    projs[me] = own[...]
+
+    group = 4
+
+    @pl.loop(0, n // group)
+    def _(c):
+        cols = pl.ds(pl.multiple_of(c * group * rank, group * rank), group * rank)
+        got = 0.5 * lax.dot_general(spread[:, cols], acts[...], TN, preferred_element_type=F32)
+        for i in range(group):
+            dsend[c * group + i] = got[i * rank : (i + 1) * rank, :].astype(BF16)
+        for i in range(group):
+            j = c * group + i
+
+            @pl.when(j != me)
+            def _():
+                send(dsend.at[j], dland.at[me], down_s, down_r, j).start()
+
+    dland[me] = dsend[me]
+
+    @pl.loop(1, n)
+    def _(s):
+        j = peer(s)
+        arrival(own, projs.at[j], proj_s, proj_r, j).wait()
+
+    ugrad[...] = jnp.zeros_like(ugrad)
+
+    @pl.loop(0, n)
+    def _(j):
+        both = projs[j].astype(F32)
+        for u in range(SLOTS):
+            keep = jnp.where(place[SLOTS * j + u] == me, 0.5, 0.0)
+            mine = (both[:, u * rank : (u + 1) * rank] * keep).astype(BF16)
+            ugrad[...] += lax.dot_general(mine, grads[tile(j, u), :], TN,
+                                          preferred_element_type=F32)
+
+    def place_out(j):
+        cols = pl.ds(pl.multiple_of(j * slab, slab), slab)
+        out[:, cols] = landed[j]
+
+    def place_down(j):
+        cols = pl.ds(pl.multiple_of(j * slab, slab), slab)
+        dgrad[:, cols] = dland[j].astype(F32)
+
+    place_out(me)
+    place_down(me)
+
+    @pl.loop(1, n)
+    def _(s):
+        j = lax.rem(me + n - s, n)
+        arrival(stage.at[j], landed.at[j], out_s, out_r, j).wait()
+        place_out(j)
+
+    @pl.loop(1, n)
+    def _(s):
+        j = lax.rem(me + n - s, n)
+        arrival(dsend.at[j], dland.at[j], down_s, down_r, j).wait()
+        place_down(j)
+
+
+def fused(n, unit_place, acts_slab, grads_all, weight, up_all, down_slabs):
+    tokens, slab = acts_slab.shape
+    out_width = grads_all.shape[1]
+    rank = up_all.shape[1]
+    rows = tokens // n
+    unit_rows = rows // SLOTS
+    vmem = pl.BlockSpec(memory_space=pltpu.VMEM)
+    dma = pltpu.SemaphoreType.DMA((n,))
+    return pl.pallas_call(
+        functools.partial(fused_kernel, n, unit_rows),
+        in_specs=[pl.BlockSpec(memory_space=pltpu.SMEM)] + [vmem] * 5,
+        out_specs=[vmem] * 3,
+        out_shape=[
+            jax.ShapeDtypeStruct((rows, n * slab), BF16),
+            jax.ShapeDtypeStruct((rank, n * slab), F32),
+            jax.ShapeDtypeStruct((rank, out_width), F32),
+        ],
+        scratch_shapes=[
+            pltpu.VMEM((n, unit_rows, SLOTS * rank), F32),
+            pltpu.VMEM((n, unit_rows, SLOTS * rank), F32),
+            pltpu.VMEM((unit_rows, SLOTS * rank), BF16),
+            pltpu.VMEM((n, unit_rows, SLOTS * rank), BF16),
+            pltpu.VMEM((n, rows, slab), BF16),
+            pltpu.VMEM((n, rows, slab), BF16),
+            pltpu.VMEM((tokens, n * rank), BF16),
+            pltpu.VMEM((n, rank, slab), BF16),
+            pltpu.VMEM((n, rank, slab), BF16),
+        ] + [dma] * 8,
+        compiler_params=pltpu.CompilerParams(
+            collective_id=0, has_side_effects=True, vmem_limit_bytes=52 * 2**20),
+        cost_estimate=pl.CostEstimate(
+            flops=2 * tokens * slab * out_width * 4, bytes_accessed=30 * 2**20, transcendentals=0),
+    )(unit_place, acts_slab, grads_all, weight, up_all, down_slabs)
 
 
 def shards(
@@ -70,7 +254,9 @@
     unit_rows = token_rows // SLOTS
     slab = row_extent // n
     tokens = token_rows * n
-    unit_place = adapter_position[token_adapter_index[::unit_rows, 0]]
+    unit_adapter = token_adapter_index.reshape(-1, unit_rows)[:, :1]
+    every = jnp.arange(adapter_position.shape[0], dtype=jnp.int32)[None, :]
+    unit_place = jnp.sum(jnp.where(unit_adapter == every, adapter_position[None, :], 0), axis=1)
 
     grads_all = lax.all_gather(output_gradient, "dp", axis=0, tiled=True)
     up_all = lax.all_gather(adapter_up_weight.transpose(0, 2, 1), "dp", axis=0, tiled=True)
@@ -85,6 +271,14 @@
     weight = (codes * scale_rows[:, :, None]).astype(BF16).reshape(slab, out_width)
 
     adapters = up_all.shape[0]
+    if grads_all.size <= 4 * 2**20 and slab % BLK == 0 and adapters == n:
+        input_gradient, down_t, up_t = fused(
+            n, unit_place, acts_slab, grads_all, weight, up_all, down_slabs)
+        return (
+            input_gradient,
+            down_t[None].transpose(0, 2, 1),
+            up_t[None].transpose(0, 2, 1),
+        )
     rows = 2 * token_rows
     whole = lambda *shape: pl.BlockSpec(shape, lambda i, place: (0,) * len(shape))
     out, proj_part, summed = pl.pallas_call(

time: 376 us -> 317 us (0.84)
  the two profiles are of different devices: /device:TPU:0 before, /device:TPU:13 now
where the time goes in v1:
time: 317 us; the launch traced here: 316 us
  Pallas kernels  113 us (36%)
  waiting for transfers between devices  88.7 us (28%)
  other arithmetic  46.1 us (15%)
  local copies, waits for them, and re-layouts  42.5 us (13%)
  between operations  14.1 us (4%)
  starting transfers between devices  11.8 us (4%)
    pallas_call x1, Pallas kernels, fused(): pl.pallas_call(functools.partial(fused_kernel, n, unit_rows), in_specs=[p...  113 us
    unnamed x2, other arithmetic  45.2 us
    all_to_all x1, waiting for transfers between devices, shards(): lax.all_to_all(acts, 'dp', split_axis=1, concat_axis=0, tiled=True)  44.9 us
    all_to_all x1, waiting for transfers between devices, shards(): lax.all_to_all(adapter_down_weight.transpose(0, 2, 1), 'dp', split_axis=2...  42.4 us
    unnamed x21, local copies, waits for them, and re-layouts  35.7 us
    all_to_all x1, starting transfers between devices, shards(): lax.all_to_all(adapter_down_weight.transpose(0, 2, 1), 'dp', split_axis=2...  6.57 us
  transfers between devices with their start and end apart: 4, of which 2 were waited for; matrix products, arithmetic and copies ran while one was open for 26% of the time, Pallas kernels for 0%

profile of v1, /device:TPU:13, one launch (start us, length us, event | category | flops | bytes accessed | tf_op | source)
XLA Modules:
  0.0 315.6 jit_solution(7926452979270157613)
XLA Ops:
  7.2 0.0 all-gather.5.cloned.1.call-start
  7.2 0.7 all-gather.5.cloned.1.call-update
  7.9 0.0 all-gather.3.cloned.1.call-start
  7.9 0.7 all-gather.3.cloned.1.call-update
  8.6 9.2 %copy.27 = bf16[1,8192,64]{2,0,1:T(2,128)(2,1)} copy(bf16[1,8192,64]{1,2,0:T(8,128)(2,1)} %param.12) | data formatting | bytes 2097152 | tf_op args[4]
  17.8 8.4 %bitcast_bitcast_fusion = bf16[8192,1,64]{2,1,0:T(2,128)(2,1)} fusion(bf16[1,8192,64]{2,0,1:T(2,128)(2,1)} %copy.27), kind=kLoop, calls=%fused_computation.12 | loop fusion | bytes 2097152
  26.3 0.5 broadcast.81
  26.8 45.2 %reduce.1 = bf16[8192,64]{1,0:T(8,128)(2,1)S(1)} reduce(bf16[8192,1,64]{2,1,0:T(2,128)(2,1)} %bitcast_bitcast_fusion, bf16[]{:T(256)} %broadcast.81), dimensions={1}, to_apply=%bitcast_bitcast_fusion.reduce_sub_computation | reduce | bytes 2097154
  72.0 2.2 reshape.89
  74.2 6.6 %all-to-all-start.1 = ((bf16[16,2,16384]{2,1,0:T(2,128)(2,1)}), bf16[16,2,16384]{2,1,0:T(2,128)(2,1)S(1)}, u32[]{:S(2)}, u32[]{:S(2)}) async-start(bf16[16,2,16384]{2,1,0:T(2,128)(2,1)} %reshape.89), calls=%async_computation.1 | async-start | bytes 2097152 | tf_op jit(solution)/shard_map/all_to_all | solution.py:263
  80.8 3.5 %copy.38 = bf16[20,16,8,512]{3,2,0,1:T(8,128)(2,1)} copy(bf16[20,16,8,512]{3,2,1,0:T(8,128)(2,1)} %bitcast.35) | data formatting | bytes 5242880 | tf_op jit(solution)/shard_map/all_to_all | solution.py:266
  84.3 42.4 %all-to-all-done.1 = bf16[16,2,16384]{2,1,0:T(2,128)(2,1)S(1)} async-done(((bf16[16,2,16384]{2,1,0:T(2,128)(2,1)}), bf16[16,2,16384]{2,1,0:T(2,128)(2,1)S(1)}, u32[]{:S(2)}, u32[]{:S(2)}) %all-to-all-start.1) | async-done | bytes 1048608 | tf_op jit(solution)/shard_map/all_to_all | solution.py:263
  126.7 0.0 copy-start.3
  126.7 0.0 copy-start.2
  126.7 0.0 copy-start.4
  126.7 5.1 %all-to-all-start = ((bf16[160,16,512]{2,0,1:T(8,128)(2,1)}), bf16[160,16,512]{2,0,1:T(8,128)(2,1)}, u32[]{:S(2)}, u32[]{:S(2)}) async-start(bf16[160,16,512]{2,0,1:T(8,128)(2,1)} %bitcast.29), calls=%async_computation | async-start | bytes 5242880 | tf_op jit(solution)/shard_map/all_to_all | solution.py:266
  131.9 0.0 copy-start.1
  131.9 0.0 copy-done.3
  131.9 0.1 copy.26
  132.0 0.0 copy-done.2
  132.0 0.1 reshape.78
  132.1 0.1 copy.33
  132.2 1.0 gather_fusion
  133.3 0.0 copy-done.4
  133.3 0.1 select_reduce_fusion.place
  133.4 0.6 mul.15
  134.0 0.0 copy-done.1
  134.0 0.7 fusion.weight
  134.7 7.0 %reshape.90 = bf16[8192,1,64]{2,1,0:T(2,128)(2,1)} reshape(bf16[16,2,16384]{2,1,0:T(2,128)(2,1)S(1)} %all-to-all-done.1) | data formatting | bytes 2097152
  141.7 2.5 copy.32
  144.1 1.6 copy.29
  145.8 0.0 all-gather.5.cloned.1.call-done.up
  145.8 44.9 %all-to-all-done = bf16[160,16,512]{2,0,1:T(8,128)(2,1)} async-done(((bf16[160,16,512]{2,0,1:T(8,128)(2,1)}), bf16[160,16,512]{2,0,1:T(8,128)(2,1)}, u32[]{:S(2)}, u32[]{:S(2)}) %all-to-all-start) | async-done | bytes 2621472 | tf_op jit(solution)/shard_map/all_to_all | solution.py:266
  190.6 0.0 all-gather.3.cloned.1.call-done.grads
  190.6 112.5 %shard_map.103 = (bf16[160,8192]{1,0:T(8,128)(2,1)}, f32[64,8192]{1,0:T(8,128)}, f32[64,1024]{1,0:T(8,128)S(1)}) custom-call(s32[32]{0:T(128)S(1)} %select_reduce_fusion.place, bf16[2560,512]{1,0:T(8,128)(2,1)} %bitcast.2.acts, bf16[2560,1024]{1,0:T(8,128)(2,1)} %all-gather.3.cloned.1.call-done.grads, bf16[512,1024]{1,0:T(8,128)(2,1)S(1)} %fusion.weight, ...), custom_call_target="tpu_custom_call" | custom-call | flops 10737418240 | bytes 31457280 | tf_op jit(solution)/shard_map/pallas_call | solution.py:212
  303.2 0.0 copy-start
  303.2 3.6 %copy.42 = bf16[160,8192]{1,0:T(8,128)(2,1)} copy(bf16[160,8192]{1,0:T(8,128)(2,1)} %get-tuple-element.12) | data formatting | bytes 5242880
  306.8 0.0 copy-done
  306.8 1.3 copy.43
  308.1 0.7 copy.44
  (3 shorter events, 0.1 us)
Async XLA Ops:
  7.2 138.6 %all-gather.5.cloned.1.call-start = ((), (), s32[]{:S(2)}) async-start(), calls=%async_computation.3 | async-start | bytes 2228224 | tf_op jit(solution)/shard_map/all_gather | solution.py:262
  7.9 182.7 %all-gather.3.cloned.1.call-start = ((), (), s32[]{:S(2)}) async-start(), calls=%async_computation.2 | async-start | bytes 5570560 | tf_op jit(solution)/shard_map/all_gather | solution.py:261
  74.2 52.5 %all-to-all-start.1 = ((bf16[16,2,16384]{2,1,0:T(2,128)(2,1)}), bf16[16,2,16384]{2,1,0:T(2,128)(2,1)S(1)}, u32[]{:S(2)}, u32[]{:S(2)}) async-start(bf16[16,2,16384]{2,1,0:T(2,128)(2,1)} %reshape.89), calls=%async_computation.1 | async-start | bytes 2097152 | tf_op jit(solution)/shard_map/all_to_all | solution.py:263
  126.7 5.1 %copy-start.3 = (f32[64,8]{0,1:T(8,128)S(1)}, f32[64,8]{0,1:T(8,128)}, u32[]{:S(2)}) copy-start(f32[64,8]{0,1:T(8,128)} %param.11) | copy-start | bytes 6148
  126.7 5.2 %copy-start.2 = (s32[2560,1]{0,1:T(1,128)S(1)}, s32[2560,1]{0,1:T(1,128)}, u32[]{:S(2)}) copy-start(s32[2560,1]{0,1:T(1,128)} %param.14) | copy-start | bytes 30724
  126.7 6.5 %copy-start.4 = (s32[16]{0:T(128)S(1)}, s32[16]{0:T(128)}, u32[]{:S(2)}) copy-start(s32[16]{0:T(128)} %param.15) | copy-start | bytes 196
  126.7 63.9 %all-to-all-start = ((bf16[160,16,512]{2,0,1:T(8,128)(2,1)}), bf16[160,16,512]{2,0,1:T(8,128)(2,1)}, u32[]{:S(2)}, u32[]{:S(2)}) async-start(bf16[160,16,512]{2,0,1:T(8,128)(2,1)} %bitcast.29), calls=%async_computation | async-start | bytes 5242880 | tf_op jit(solution)/shard_map/all_to_all | solution.py:266
  131.9 2.1 copy-start.1
  303.2 3.6 %copy-start = (f32[64,8192]{1,0:T(8,128)S(1)}, f32[64,8192]{1,0:T(8,128)}, u32[]{:S(2)}) copy-start(f32[64,8192]{1,0:T(8,128)} %get-tuple-element.7) | copy-start | bytes 6291460
Sparse Core Ops, SparseCore 0:
  10.2 41.0 all-gather.4
  53.5 71.2 all-gather.2

commit v2 on v1

--- a/solution.py
+++ b/solution.py
@@ -52,7 +52,77 @@
         )
 
 
-def fused_kernel(n, unit_rows, place, acts, grads, weight, up, down, out, dgrad, ugrad,
+def exchange_kernel(n, acts, down, acts_out, down_out, acts_s, acts_r, down_s, down_r, local):
+    me = lax.axis_index("dp")
+    rows = acts.shape[0]
+    slab = acts.shape[1] // n
+
+    def peer(s):
+        return lax.rem(me + s, n)
+
+    def cols(j):
+        return pl.ds(pl.multiple_of(j * slab, slab), slab)
+
+    def lines(j):
+        return pl.ds(pl.multiple_of(j * rows, 16), rows)
+
+    def remote(src, dst, send_sem, recv_sem, j):
+        return pltpu.make_async_remote_copy(
+            src_ref=src, dst_ref=dst, send_sem=send_sem, recv_sem=recv_sem,
+            device_id={"dp": j}, device_id_type=pl.DeviceIdType.MESH)
+
+    mine = pltpu.make_async_copy(acts.at[:, cols(me)], acts_out.at[lines(me), :], local.at[0])
+    own = pltpu.make_async_copy(down.at[:, cols(me)], down_out.at[me], local.at[1])
+    mine.start()
+    own.start()
+    barrier = pltpu.get_barrier_semaphore()
+
+    @pl.loop(1, n)
+    def _(s):
+        pl.semaphore_signal(barrier, inc=1, device_id={"dp": peer(s)},
+                            device_id_type=pl.DeviceIdType.MESH)
+
+    pl.semaphore_wait(barrier, n - 1)
+
+    @pl.loop(1, n)
+    def _(s):
+        j = peer(s)
+        remote(down.at[:, cols(j)], down_out.at[me], down_s.at[j], down_r.at[me], j).start()
+        remote(acts.at[:, cols(j)], acts_out.at[lines(me), :], acts_s.at[j], acts_r.at[me],
+               j).start()
+
+    mine.wait()
+    own.wait()
+
+    @pl.loop(1, n)
+    def _(s):
+        j = lax.rem(me + n - s, n)
+        remote(down.at[:, cols(j)], down_out.at[j], down_s.at[j], down_r.at[j], j).wait()
+        remote(acts.at[:, cols(j)], acts_out.at[lines(j), :], acts_s.at[j], acts_r.at[j],
+               j).wait()
+
+
+def exchange(n, acts, down_t):
+    rows, width = acts.shape
+    slab = width // n
+    dma = pltpu.SemaphoreType.DMA((n,))
+    anywhere = pl.BlockSpec(memory_space=pl.ANY)
+    return pl.pallas_call(
+        functools.partial(exchange_kernel, n),
+        in_specs=[anywhere] * 2,
+        out_specs=[anywhere] * 2,
+        out_shape=[
+            jax.ShapeDtypeStruct((n * rows, slab), BF16),
+            jax.ShapeDtypeStruct((n, down_t.shape[0], slab), BF16),
+        ],
+        scratch_shapes=[dma] * 4 + [pltpu.SemaphoreType.DMA((2,))],
+        compiler_params=pltpu.CompilerParams(collective_id=1, has_side_effects=True),
+        cost_estimate=pl.CostEstimate(
+            flops=0, bytes_accessed=200 * 2**20, transcendentals=0),
+    )(acts, down_t)
+
+
+def fused_kernel(n, unit_rows, place, acts, both_all, weight, down, out, dgrad, ugrad,
                  part, part_in, own, projs, stage, landed, spread, dsend, dland,
                  part_s, part_r, proj_s, proj_r, out_s, out_r, down_s, down_r):
     me = lax.axis_index("dp")
@@ -83,6 +153,12 @@
 
     pl.semaphore_wait(barrier, n - 1)
 
+    def grad_tile(j, u):
+        return both_all[j, pl.ds(u * unit_rows, unit_rows), :]
+
+    def up_of(p):
+        return both_all[p, pl.ds(rows, rank), :]
+
     def tile(j, u):
         return pl.ds(pl.multiple_of(j * rows + u * unit_rows, 16), unit_rows)
 
@@ -92,7 +168,7 @@
                             preferred_element_type=F32)
             for u in range(SLOTS)
         ]
-        dst[j] = jnp.concatenate(both, axis=1)
+        dst[j] = jnp.concatenate(both, axis=1).astype(BF16)
 
     @pl.loop(1, n)
     def _(s):
@@ -108,8 +184,8 @@
         for u in range(SLOTS):
             at = tile(j, u)
             p = place[SLOTS * j + u]
-            g = grads[at, :]
-            low = lax.dot_general(g, up[p], NT, preferred_element_type=F32).astype(BF16)
+            g = grad_tile(j, u)
+            low = lax.dot_general(g, up_of(p), NT, preferred_element_type=F32).astype(BF16)
             base = lax.dot_general(g, weight[...], NT, preferred_element_type=F32)
             back = (0.5 * jnp.dot(low, down[p], preferred_element_type=F32)).astype(BF16)
             dst[j, pl.ds(u * unit_rows, unit_rows), :] = (base + back.astype(F32)).astype(BF16)
@@ -132,9 +208,9 @@
         j = peer(s)
         arrival(part.at[j], part_in.at[j], part_s, part_r, j).wait()
 
-    total = part_in[0]
+    total = part_in[0].astype(F32)
     for j in range(1, n):
-        total = total + part_in[j]
+        total = total + part_in[j].astype(F32)
     own[...] = total.astype(BF16)
 
     @pl.loop(1, n)
@@ -174,7 +250,7 @@
         for u in range(SLOTS):
             keep = jnp.where(place[SLOTS * j + u] == me, 0.5, 0.0)
             mine = (both[:, u * rank : (u + 1) * rank] * keep).astype(BF16)
-            ugrad[...] += lax.dot_general(mine, grads[tile(j, u), :], TN,
+            ugrad[...] += lax.dot_general(mine, grad_tile(j, u), TN,
                                           preferred_element_type=F32)
 
     def place_out(j):
@@ -201,17 +277,17 @@
         place_down(j)
 
 
-def fused(n, unit_place, acts_slab, grads_all, weight, up_all, down_slabs):
+def fused(n, unit_place, acts_slab, both_all, weight, down_slabs):
     tokens, slab = acts_slab.shape
-    out_width = grads_all.shape[1]
-    rank = up_all.shape[1]
+    out_width = both_all.shape[2]
+    rank = down_slabs.shape[1]
     rows = tokens // n
     unit_rows = rows // SLOTS
     vmem = pl.BlockSpec(memory_space=pltpu.VMEM)
     dma = pltpu.SemaphoreType.DMA((n,))
     return pl.pallas_call(
         functools.partial(fused_kernel, n, unit_rows),
-        in_specs=[pl.BlockSpec(memory_space=pltpu.SMEM)] + [vmem] * 5,
+        in_specs=[pl.BlockSpec(memory_space=pltpu.SMEM)] + [vmem] * 4,
         out_specs=[vmem] * 3,
         out_shape=[
             jax.ShapeDtypeStruct((rows, n * slab), BF16),
@@ -219,8 +295,8 @@
             jax.ShapeDtypeStruct((rank, out_width), F32),
         ],
         scratch_shapes=[
-            pltpu.VMEM((n, unit_rows, SLOTS * rank), F32),
-            pltpu.VMEM((n, unit_rows, SLOTS * rank), F32),
+            pltpu.VMEM((n, unit_rows, SLOTS * rank), BF16),
+            pltpu.VMEM((n, unit_rows, SLOTS * rank), BF16),
             pltpu.VMEM((unit_rows, SLOTS * rank), BF16),
             pltpu.VMEM((n, unit_rows, SLOTS * rank), BF16),
             pltpu.VMEM((n, rows, slab), BF16),
@@ -233,7 +309,7 @@
             collective_id=0, has_side_effects=True, vmem_limit_bytes=52 * 2**20),
         cost_estimate=pl.CostEstimate(
             flops=2 * tokens * slab * out_width * 4, bytes_accessed=30 * 2**20, transcendentals=0),
-    )(unit_place, acts_slab, grads_all, weight, up_all, down_slabs)
+    )(unit_place, acts_slab, both_all, weight, down_slabs)
 
 
 def shards(
@@ -258,27 +334,29 @@
     every = jnp.arange(adapter_position.shape[0], dtype=jnp.int32)[None, :]
     unit_place = jnp.sum(jnp.where(unit_adapter == every, adapter_position[None, :], 0), axis=1)
 
-    grads_all = lax.all_gather(output_gradient, "dp", axis=0, tiled=True)
-    up_all = lax.all_gather(adapter_up_weight.transpose(0, 2, 1), "dp", axis=0, tiled=True)
-    down_slabs = lax.all_to_all(
-        adapter_down_weight.transpose(0, 2, 1), "dp", split_axis=2, concat_axis=0, tiled=True
-    )
-    acts_slab = lax.all_to_all(acts, "dp", split_axis=1, concat_axis=0, tiled=True)
-
+    up_t = adapter_up_weight.transpose(0, 2, 1)
+    down_t = adapter_down_weight.transpose(0, 2, 1)
     row_ids = me * slab + jnp.arange(slab, dtype=jnp.int32)
     scale_rows = weight_block_scale[row_ids // BLK]
     codes = frozen_weight_codes.astype(F32).reshape(slab, out_width // BLK, BLK)
     weight = (codes * scale_rows[:, :, None]).astype(BF16).reshape(slab, out_width)
 
-    adapters = up_all.shape[0]
-    if grads_all.size <= 4 * 2**20 and slab % BLK == 0 and adapters == n:
-        input_gradient, down_t, up_t = fused(
-            n, unit_place, acts_slab, grads_all, weight, up_all, down_slabs)
+    adapters = n * up_t.shape[0]
+    if tokens * out_width <= 4 * 2**20 and slab % BLK == 0 and adapters == n:
+        both = jnp.concatenate([output_gradient, up_t[0]], axis=0)
+        both_all = lax.all_gather(both, "dp", axis=0, tiled=True).reshape(n, -1, out_width)
+        acts_slab, down_slabs = exchange(n, acts, down_t[0])
+        input_gradient, down_out, up_out = fused(
+            n, unit_place, acts_slab, both_all, weight, down_slabs)
         return (
             input_gradient,
-            down_t[None].transpose(0, 2, 1),
-            up_t[None].transpose(0, 2, 1),
+            down_out[None].transpose(0, 2, 1),
+            up_out[None].transpose(0, 2, 1),
         )
+    grads_all = lax.all_gather(output_gradient, "dp", axis=0, tiled=True)
+    up_all = lax.all_gather(up_t, "dp", axis=0, tiled=True)
+    down_slabs = lax.all_to_all(down_t, "dp", split_axis=2, concat_axis=0, tiled=True)
+    acts_slab = lax.all_to_all(acts, "dp", split_axis=1, concat_axis=0, tiled=True)
     rows = 2 * token_rows
     whole = lambda *shape: pl.BlockSpec(shape, lambda i, place: (0,) * len(shape))
     out, proj_part, summed = pl.pallas_call(

time: 317 us -> 262 us (0.83)
  Pallas kernels: 113 us -> 235 us
  waiting for transfers between devices: 88.7 us -> 0.04 us
  other arithmetic: 46.1 us -> 3.41 us
  local copies, waits for them, and re-layouts: 42.5 us -> 8.74 us
  starting transfers between devices: 11.8 us -> 0.04 us
    pallas_call x0 -> x1, Pallas kernels: none -> 129 us  [exchange(): pl.pallas_call(functools.partial(exchange_kernel, n), in_specs=[anywhere]...]
    all_to_all x2 -> x0, waiting for transfers between devices: 87.3 us -> none  [the longest x1 44.9 us: shards(): lax.all_to_all(acts, 'dp', split_axis=1, concat_axis=0, tiled=True)]
    unnamed x2 -> x1, other arithmetic: 45.2 us -> 0.73 us
    unnamed x21 -> x11, local copies, waits for them, and re-layouts: 35.7 us -> 7.03 us
    all_to_all x2 -> x0, starting transfers between devices: 11.7 us -> none  [the longest x1 6.57 us: shards(): lax.all_to_all(adapter_down_weight.transpose(0, 2, 1), 'dp', split_axis=2...]
    pallas_call x1, Pallas kernels: 113 us -> 106 us  [fused(): pl.pallas_call(functools.partial(fused_kernel, n, unit_rows), in_specs=[p...]
    all_to_all x2 -> x0, local copies, waits for them, and re-layouts: 5.13 us -> none  [the longest x1 3.51 us: shards(): lax.all_to_all(acts, 'dp', split_axis=1, concat_axis=0, tiled=True)]
  transfers between devices with their start and end apart: 4 -> 1, of which waited for: 2 -> 0; matrix products, arithmetic and copies ran while one was open for 26% -> 2% of each run, Pallas kernels for 0% -> 49%
where the time goes in v2:
time: 262 us; the launch traced here: 261 us
  Pallas kernels  235 us (90%)
  between operations  14.1 us (5%)
  local copies, waits for them, and re-layouts  8.74 us (3%)
  other arithmetic  3.41 us (1%)
    pallas_call x1, Pallas kernels, exchange(): pl.pallas_call(functools.partial(exchange_kernel, n), in_specs=[anywhere]...  129 us
    pallas_call x1, Pallas kernels, fused(): pl.pallas_call(functools.partial(fused_kernel, n, unit_rows), in_specs=[p...  106 us
    unnamed x11, local copies, waits for them, and re-layouts  7.03 us
  transfers between devices with their start and end apart: 1, of which 0 were waited for; matrix products, arithmetic and copies ran while one was open for 2% of the time, Pallas kernels for 49%

profile of v2, /device:TPU:13, one launch (start us, length us, event | category | flops | bytes accessed | tf_op | source)
XLA Modules:
  0.0 261.3 jit_solution(2032617712422992903)
XLA Ops:
  7.2 0.0 all-gather.2.cloned.1.call-start
  7.2 1.8 pad_maximum_fusion
  9.1 0.0 all-gather.2.cloned.1.call-update
  9.1 0.7 reduce
  9.8 0.1 reshape.78
  9.9 0.1 copy.17
  10.0 0.8 copy.16
  10.8 1.0 gather_fusion
  11.8 0.0 copy-start.2
  11.8 129.2 %shard_map.103 = (bf16[2560,512]{1,0:T(8,128)(2,1)}, bf16[16,64,512]{2,1,0:T(8,128)(2,1)}) custom-call(bf16[160,8192]{1,0:T(8,128)(2,1)} %acts.1, bf16[64,8192]{1,0:T(8,128)(2,1)} %bitcast.24), custom_call_target="tpu_custom_call" | custom-call | bytes 209715200 | tf_op jit(solution)/shard_map/pallas_call | solution.py:110
  141.0 0.0 copy-start.1
  141.0 0.0 copy-done.2
  141.0 0.1 select_reduce_fusion.place
  141.1 0.6 mul.15
  141.7 0.5 copy-done.1
  142.2 0.7 fusion.weight
  143.0 0.0 all-gather.2.cloned.1.call-done
  143.0 105.8 %shard_map.104 = (bf16[160,8192]{1,0:T(8,128)(2,1)}, f32[64,8192]{1,0:T(8,128)}, f32[64,1024]{1,0:T(8,128)S(1)}) custom-call(s32[32]{0:T(128)S(1)} %select_reduce_fusion.place, bf16[2560,512]{1,0:T(8,128)(2,1)} %get-tuple-element.8.acts, bf16[16,224,1024]{2,1,0:T(8,128)(2,1)} %bitcast.29, bf16[512,1024]{1,0:T(8,128)(2,1)S(1)} %fusion.weight, ...), custom_call_target="tpu_custom_call" | custom-call | flops 10737418240 | bytes 31457280 | tf_op jit(solution)/shard_map/pallas_call | solution.py:288
  248.8 0.0 copy-start
  248.8 3.6 %copy.23 = bf16[160,8192]{1,0:T(8,128)(2,1)} copy(bf16[160,8192]{1,0:T(8,128)(2,1)} %get-tuple-element.16) | data formatting | bytes 5242880
  252.4 0.0 copy-done
  252.4 1.3 copy.24
  253.8 0.7 copy.25
  (2 shorter events, 0.0 us)
Async XLA Ops:
  7.2 135.8 %all-gather.2.cloned.1.call-start = ((), (), s32[]{:S(2)}) async-start(), calls=%async_computation | async-start | bytes 7798784 | tf_op jit(solution)/shard_map/all_gather | solution.py:347
  11.8 129.2 %copy-start.2 = (s32[16]{0:T(128)S(1)}, s32[16]{0:T(128)}, u32[]{:S(2)}) copy-start(s32[16]{0:T(128)} %param.15) | copy-start | bytes 196
  141.0 1.2 copy-start.1
  248.8 3.6 %copy-start = (f32[64,8192]{1,0:T(8,128)S(1)}, f32[64,8192]{1,0:T(8,128)}, u32[]{:S(2)}) copy-start(f32[64,8192]{1,0:T(8,128)} %get-tuple-element.11) | copy-start | bytes 6291460
Sparse Core Ops, SparseCore 0:
  10.9 124.0 all-gather.1

commit v3 on v2

--- a/solution.py
+++ b/solution.py
@@ -9,6 +9,7 @@
 
 BLK = 128
 SLOTS = 2
+PLANE = 4
 NT = (((1,), (1,)), ((), ()))
 TN = (((0,), (0,)), ((), ()))
 F32 = jnp.float32
@@ -52,7 +53,8 @@
         )
 
 
-def exchange_kernel(n, acts, down, acts_out, down_out, acts_s, acts_r, down_s, down_r, local):
+def exchange_kernel(n, acts, down, both, acts_out, down_out, gathered, acts_s, acts_r, down_s,
+                    down_r, up_s, low_s, side_s, core_s, got_r, local):
     me = lax.axis_index("dp")
     rows = acts.shape[0]
     slab = acts.shape[1] // n
@@ -75,6 +77,8 @@
     own = pltpu.make_async_copy(down.at[:, cols(me)], down_out.at[me], local.at[1])
     mine.start()
     own.start()
+    first = pltpu.make_async_copy(both, gathered.at[me], local.at[2])
+    first.start()
     barrier = pltpu.get_barrier_semaphore()
 
     @pl.loop(1, n)
@@ -83,13 +87,83 @@
                             device_id_type=pl.DeviceIdType.MESH)
 
     pl.semaphore_wait(barrier, n - 1)
+    first.wait()
+
+    planes = n // PLANE
+    z, q = lax.div(me, PLANE), lax.rem(me, PLANE)
+    side_q = lax.rem(q + PLANE // 2, PLANE)
+    core_q = q + 1 - 2 * lax.rem(q, 2)
+    far_q = lax.rem(core_q + PLANE // 2, PLANE)
+    side, core = z * PLANE + side_q, z * PLANE + core_q
+
+    def hand(b, j, sems):
+        return remote(gathered.at[b], gathered.at[b], sems.at[b], got_r.at[b], j)
+
+    def spread(b, upward, downward):
+        if upward:
+            @pl.when(z + 1 < planes)
+            def _():
+                hand(b, me + PLANE, up_s).start()
+        if downward:
+            @pl.when(z >= 1)
+            def _():
+                hand(b, me - PLANE, low_s).start()
+        hand(b, side, side_s).start()
+        hand(b, core, core_s).start()
+
+    def send_acts(lo, hi):
+        @pl.loop(lo, hi)
+        def _(s):
+            j = peer(s)
+            remote(acts.at[:, cols(j)], acts_out.at[lines(me), :], acts_s.at[j], acts_r.at[me],
+                   j).start()
+
+    spread(me, True, True)
 
     @pl.loop(1, n)
     def _(s):
         j = peer(s)
         remote(down.at[:, cols(j)], down_out.at[me], down_s.at[j], down_r.at[me], j).start()
-        remote(acts.at[:, cols(j)], acts_out.at[lines(me), :], acts_s.at[j], acts_r.at[me],
-               j).start()
+
+    cuts = [1 + (n - 1) * k // planes for k in range(planes + 1)]
+    send_acts(cuts[0], cuts[1])
+    for k in range(1, planes):
+        @pl.when(z >= k)
+        def _():
+            b = (z - k) * PLANE + q
+            hand(b, core, core_s).wait_recv()
+            spread(b, True, False)
+
+        @pl.when(z + k < planes)
+        def _():
+            b = (z + k) * PLANE + q
+            hand(b, core, core_s).wait_recv()
+            spread(b, False, True)
+
+        send_acts(cuts[k], cuts[k + 1])
+
+    @pl.loop(0, planes)
+    def _(zz):
+        b = zz * PLANE + side_q
+        hand(b, core, core_s).wait_recv()
+        hand(b, core, core_s).start()
+
+    @pl.loop(0, planes)
+    def _(zz):
+        hand(zz * PLANE + core_q, core, core_s).wait_recv()
+        hand(zz * PLANE + far_q, core, core_s).wait_recv()
+        hand(zz * PLANE + side_q, core, core_s).wait_send()
+        b = zz * PLANE + q
+        hand(b, core, core_s).wait_send()
+        hand(b, side, side_s).wait_send()
+
+        @pl.when((z + 1 < planes) & (zz <= z))
+        def _():
+            hand(b, me + PLANE, up_s).wait_send()
+
+        @pl.when((z >= 1) & (zz >= z))
+        def _():
+            hand(b, me - PLANE, low_s).wait_send()
 
     mine.wait()
     own.wait()
@@ -102,24 +176,25 @@
                j).wait()
 
 
-def exchange(n, acts, down_t):
+def exchange(n, acts, down_t, both):
     rows, width = acts.shape
     slab = width // n
     dma = pltpu.SemaphoreType.DMA((n,))
     anywhere = pl.BlockSpec(memory_space=pl.ANY)
     return pl.pallas_call(
         functools.partial(exchange_kernel, n),
-        in_specs=[anywhere] * 2,
-        out_specs=[anywhere] * 2,
+        in_specs=[anywhere] * 3,
+        out_specs=[anywhere] * 3,
         out_shape=[
             jax.ShapeDtypeStruct((n * rows, slab), BF16),
             jax.ShapeDtypeStruct((n, down_t.shape[0], slab), BF16),
+            jax.ShapeDtypeStruct((n, *both.shape), BF16),
         ],
-        scratch_shapes=[dma] * 4 + [pltpu.SemaphoreType.DMA((2,))],
+        scratch_shapes=[dma] * 9 + [pltpu.SemaphoreType.DMA((3,))],
         compiler_params=pltpu.CompilerParams(collective_id=1, has_side_effects=True),
         cost_estimate=pl.CostEstimate(
             flops=0, bytes_accessed=200 * 2**20, transcendentals=0),
-    )(acts, down_t)
+    )(acts, down_t, both)
 
 
 def fused_kernel(n, unit_rows, place, acts, both_all, weight, down, out, dgrad, ugrad,
@@ -342,10 +417,9 @@
     weight = (codes * scale_rows[:, :, None]).astype(BF16).reshape(slab, out_width)
 
     adapters = n * up_t.shape[0]
-    if tokens * out_width <= 4 * 2**20 and slab % BLK == 0 and adapters == n:
+    if tokens * out_width <= 4 * 2**20 and slab % BLK == 0 and adapters == n and n % PLANE == 0:
         both = jnp.concatenate([output_gradient, up_t[0]], axis=0)
-        both_all = lax.all_gather(both, "dp", axis=0, tiled=True).reshape(n, -1, out_width)
-        acts_slab, down_slabs = exchange(n, acts, down_t[0])
+        acts_slab, down_slabs, both_all = exchange(n, acts, down_t[0], both)
         input_gradient, down_out, up_out = fused(
             n, unit_place, acts_slab, both_all, weight, down_slabs)
         return (

time: 262 us -> 263 us (level)
  Pallas kernels: 235 us -> 250 us
  between operations: 14.1 us -> 0.74 us
    pallas_call x1, Pallas kernels: 106 us -> 117 us  [fused(): pl.pallas_call(functools.partial(fused_kernel, n, unit_rows), in_specs=[p...]
    pallas_call x1, Pallas kernels: 129 us -> 133 us  [exchange(): pl.pallas_call(functools.partial(exchange_kernel, n), in_specs=[anywhere]...]
    unnamed x11 -> x13, local copies, waits for them, and re-layouts: 7.03 us -> 6.5 us
  transfers between devices with their start and end apart: 1 -> 0, of which waited for: 0 -> 0; matrix products, arithmetic and copies ran while one was open for 2% -> 0% of each run, Pallas kernels for 49% -> 0%
where the time goes in v3:
time: 263 us; the launch traced here: 262 us
  Pallas kernels  250 us (95%)
  local copies, waits for them, and re-layouts  8.21 us (3%)
  other arithmetic  3.09 us (1%)
    pallas_call x1, Pallas kernels, exchange(): pl.pallas_call(functools.partial(exchange_kernel, n), in_specs=[anywhere]...  133 us
    pallas_call x1, Pallas kernels, fused(): pl.pallas_call(functools.partial(fused_kernel, n, unit_rows), in_specs=[p...  117 us
    unnamed x13, local copies, waits for them, and re-layouts  6.5 us

profile of v3, /device:TPU:13, one launch (start us, length us, event | category | flops | bytes accessed | tf_op | source)
XLA Modules:
  0.0 262.4 jit_solution(2520831378739034400)
XLA Ops:
  0.6 0.0 copy-start.3
  0.6 0.0 copy-start.2
  0.7 0.8 reduce
  1.5 0.1 reshape.75
  1.6 0.1 copy.17
  1.6 0.7 select_reduce_fusion.place
  2.4 0.8 copy.16
  3.2 1.0 gather_fusion
  4.2 0.0 copy-done.3
  4.2 0.0 copy-done.2
  4.2 0.0 copy-start.1
  4.2 0.8 pad_maximum_fusion.both
  5.0 0.6 mul.15
  5.6 0.0 copy-done.1
  5.6 0.7 fusion.weight
  6.4 133.5 %shard_map.103 = (bf16[2560,512]{1,0:T(8,128)(2,1)}, bf16[16,64,512]{2,1,0:T(8,128)(2,1)}, bf16[16,224,1024]{2,1,0:T(8,128)(2,1)}) custom-call(bf16[160,8192]{1,0:T(8,128)(2,1)} %acts.1, bf16[64,8192]{1,0:T(8,128)(2,1)} %bitcast.23, bf16[224,1024]{1,0:T(8,128)(2,1)} %pad_maximum_fusion.both), custom_call_target="tpu_custom_call" | custom-call | bytes 209715200 | tf_op jit(solution)/shard_map/pallas_call | solution.py:184
  139.9 116.8 %shard_map.104 = (bf16[160,8192]{1,0:T(8,128)(2,1)}, f32[64,8192]{1,0:T(8,128)}, f32[64,1024]{1,0:T(8,128)S(1)}) custom-call(s32[32]{0:T(128)S(1)} %select_reduce_fusion.place, bf16[2560,512]{1,0:T(8,128)(2,1)} %get-tuple-element.9.acts, bf16[16,224,1024]{2,1,0:T(8,128)(2,1)} %get-tuple-element.10.both_all, bf16[512,1024]{1,0:T(8,128)(2,1)S(1)} %fusion.weight, ...), custom_call_target="tpu_custom_call" | custom-call | flops 10737418240 | bytes 31457280 | tf_op jit(solution)/shard_map/pallas_call | solution.py:363
  256.7 0.0 copy-start
  256.7 3.6 %copy.23 = bf16[160,8192]{1,0:T(8,128)(2,1)} copy(bf16[160,8192]{1,0:T(8,128)(2,1)} %get-tuple-element.18) | data formatting | bytes 5242880
  260.3 0.0 copy-done
  260.3 1.3 copy.24
  261.7 0.7 copy.25
  (2 shorter events, 0.0 us)
Async XLA Ops:
  0.6 3.6 %copy-start.3 = (bf16[1,1024,64]{1,2,0:T(8,128)(2,1)S(1)}, bf16[1,1024,64]{1,2,0:T(8,128)(2,1)}, u32[]{:S(2)}) copy-start(bf16[1,1024,64]{1,2,0:T(8,128)(2,1)} %param.13) | copy-start | bytes 393220
  0.6 3.6 %copy-start.2 = (bf16[160,1024]{1,0:T(8,128)(2,1)S(1)}, bf16[160,1024]{1,0:T(8,128)(2,1)}, u32[]{:S(2)}) copy-start(bf16[160,1024]{1,0:T(8,128)(2,1)} %param.9) | copy-start | bytes 983044
  4.2 1.4 copy-start.1
  256.7 3.6 %copy-start = (f32[64,8192]{1,0:T(8,128)S(1)}, f32[64,8192]{1,0:T(8,128)}, u32[]{:S(2)}) copy-start(f32[64,8192]{1,0:T(8,128)} %get-tuple-element.13) | copy-start | bytes 6291460

commit v4 on v3

--- a/solution.py
+++ b/solution.py
@@ -53,29 +53,22 @@
         )
 
 
-def exchange_kernel(n, acts, down, both, acts_out, down_out, gathered, acts_s, acts_r, down_s,
-                    down_r, up_s, low_s, side_s, core_s, got_r, local):
+def exchange_kernel(n, down, both, down_out, gathered, down_s, down_r, up_s, low_s, side_s, core_s, got_r, local):
     me = lax.axis_index("dp")
-    rows = acts.shape[0]
-    slab = acts.shape[1] // n
+    slab = down.shape[1] // n
 
     def peer(s):
         return lax.rem(me + s, n)
 
     def cols(j):
         return pl.ds(pl.multiple_of(j * slab, slab), slab)
-
-    def lines(j):
-        return pl.ds(pl.multiple_of(j * rows, 16), rows)
 
     def remote(src, dst, send_sem, recv_sem, j):
         return pltpu.make_async_remote_copy(
             src_ref=src, dst_ref=dst, send_sem=send_sem, recv_sem=recv_sem,
             device_id={"dp": j}, device_id_type=pl.DeviceIdType.MESH)
 
-    mine = pltpu.make_async_copy(acts.at[:, cols(me)], acts_out.at[lines(me), :], local.at[0])
     own = pltpu.make_async_copy(down.at[:, cols(me)], down_out.at[me], local.at[1])
-    mine.start()
     own.start()
     first = pltpu.make_async_copy(both, gathered.at[me], local.at[2])
     first.start()
@@ -111,13 +104,6 @@
         hand(b, side, side_s).start()
         hand(b, core, core_s).start()
 
-    def send_acts(lo, hi):
-        @pl.loop(lo, hi)
-        def _(s):
-            j = peer(s)
-            remote(acts.at[:, cols(j)], acts_out.at[lines(me), :], acts_s.at[j], acts_r.at[me],
-                   j).start()
-
     spread(me, True, True)
 
     @pl.loop(1, n)
@@ -125,8 +111,6 @@
         j = peer(s)
         remote(down.at[:, cols(j)], down_out.at[me], down_s.at[j], down_r.at[me], j).start()
 
-    cuts = [1 + (n - 1) * k // planes for k in range(planes + 1)]
-    send_acts(cuts[0], cuts[1])
     for k in range(1, planes):
         @pl.when(z >= k)
         def _():
@@ -139,8 +123,6 @@
             b = (z + k) * PLANE + q
             hand(b, core, core_s).wait_recv()
             spread(b, False, True)
-
-        send_acts(cuts[k], cuts[k + 1])
 
     @pl.loop(0, planes)
     def _(zz):
@@ -165,41 +147,37 @@
         def _():
             hand(b, me - PLANE, low_s).wait_send()
 
-    mine.wait()
     own.wait()
 
     @pl.loop(1, n)
     def _(s):
         j = lax.rem(me + n - s, n)
         remote(down.at[:, cols(j)], down_out.at[j], down_s.at[j], down_r.at[j], j).wait()
-        remote(acts.at[:, cols(j)], acts_out.at[lines(j), :], acts_s.at[j], acts_r.at[j],
-               j).wait()
-
-
-def exchange(n, acts, down_t, both):
-    rows, width = acts.shape
-    slab = width // n
+
+
+def exchange(n, down_t, both):
+    slab = down_t.shape[1] // n
     dma = pltpu.SemaphoreType.DMA((n,))
     anywhere = pl.BlockSpec(memory_space=pl.ANY)
     return pl.pallas_call(
         functools.partial(exchange_kernel, n),
-        in_specs=[anywhere] * 3,
-        out_specs=[anywhere] * 3,
+        in_specs=[anywhere] * 2,
+        out_specs=[anywhere] * 2,
         out_shape=[
-            jax.ShapeDtypeStruct((n * rows, slab), BF16),
             jax.ShapeDtypeStruct((n, down_t.shape[0], slab), BF16),
             jax.ShapeDtypeStruct((n, *both.shape), BF16),
         ],
-        scratch_shapes=[dma] * 9 + [pltpu.SemaphoreType.DMA((3,))],
+        scratch_shapes=[dma] * 7 + [pltpu.SemaphoreType.DMA((3,))],
         compiler_params=pltpu.CompilerParams(collective_id=1, has_side_effects=True),
         cost_estimate=pl.CostEstimate(
             flops=0, bytes_accessed=200 * 2**20, transcendentals=0),
-    )(acts, down_t, both)
-
-
-def fused_kernel(n, unit_rows, place, acts, both_all, weight, down, out, dgrad, ugrad,
-                 part, part_in, own, projs, stage, landed, spread, dsend, dland,
-                 part_s, part_r, proj_s, proj_r, out_s, out_r, down_s, down_r):
+    )(down_t, both)
+
+
+def fused_kernel(n, unit_rows, place, acts_own, both_all, weight, down, out, dgrad, ugrad,
+                 acts, part, part_in, own, projs, stage, landed, spread, dsend, dland,
+                 part_s, part_r, proj_s, proj_r, out_s, out_r, down_s, down_r,
+                 acts_s, acts_r, local):
     me = lax.axis_index("dp")
     rows = SLOTS * unit_rows
     slab = weight.shape[0]
@@ -245,13 +223,19 @@
         ]
         dst[j] = jnp.concatenate(both, axis=1).astype(BF16)
 
+    def acts_cols(j):
+        return acts_own.at[:, pl.ds(pl.multiple_of(j * slab, slab), slab)]
+
+    def acts_rows(j):
+        return acts.at[pl.ds(pl.multiple_of(j * rows, 16), rows), :]
+
+    mine = pltpu.make_async_copy(acts_cols(me), acts_rows(me), local.at[0])
+    mine.start()
+
     @pl.loop(1, n)
     def _(s):
         j = peer(s)
-        project(j, part)
-        send(part.at[j], part_in.at[me], part_s, part_r, j).start()
-
-    project(me, part_in)
+        send(acts_cols(j), acts_rows(me), acts_s, acts_r, j).start()
 
     lane_half = lax.broadcasted_iota(jnp.int32, (unit_rows, 2 * rank), 1) // rank
 
@@ -278,22 +262,16 @@
 
     block(me, landed)
 
-    @pl.loop(1, n)
-    def _(s):
-        j = peer(s)
-        arrival(part.at[j], part_in.at[j], part_s, part_r, j).wait()
-
-    total = part_in[0].astype(F32)
-    for j in range(1, n):
-        total = total + part_in[j].astype(F32)
-    own[...] = total.astype(BF16)
-
-    @pl.loop(1, n)
-    def _(s):
-        j = peer(s)
-        send(own, projs.at[me], proj_s, proj_r, j).start()
-
-    projs[me] = own[...]
+    mine.wait()
+
+    @pl.loop(1, n)
+    def _(s):
+        j = lax.rem(me + n - s, n)
+        arrival(acts_cols(j), acts_rows(j), acts_s, acts_r, j).wait_recv()
+        project(j, part)
+        send(part.at[j], part_in.at[me], part_s, part_r, j).start()
+
+    project(me, part_in)
 
     group = 4
 
@@ -315,6 +293,23 @@
     @pl.loop(1, n)
     def _(s):
         j = peer(s)
+        arrival(part.at[j], part_in.at[j], part_s, part_r, j).wait()
+
+    total = part_in[0].astype(F32)
+    for j in range(1, n):
+        total = total + part_in[j].astype(F32)
+    own[...] = total.astype(BF16)
+
+    @pl.loop(1, n)
+    def _(s):
+        j = peer(s)
+        send(own, projs.at[me], proj_s, proj_r, j).start()
+
+    projs[me] = own[...]
+
+    @pl.loop(1, n)
+    def _(s):
+        j = peer(s)
         arrival(own, projs.at[j], proj_s, proj_r, j).wait()
 
     ugrad[...] = jnp.zeros_like(ugrad)
@@ -342,6 +337,7 @@
     @pl.loop(1, n)
     def _(s):
         j = lax.rem(me + n - s, n)
+        arrival(acts_cols(j), acts_rows(j), acts_s, acts_r, j).wait_send()
         arrival(stage.at[j], landed.at[j], out_s, out_r, j).wait()
         place_out(j)
 
@@ -352,8 +348,9 @@
         place_down(j)
 
 
-def fused(n, unit_place, acts_slab, both_all, weight, down_slabs):
-    tokens, slab = acts_slab.shape
+def fused(n, unit_place, acts, both_all, weight, down_slabs):
+    slab = acts.shape[1] // n
+    tokens = acts.shape[0] * n
     out_width = both_all.shape[2]
     rank = down_slabs.shape[1]
     rows = tokens // n
@@ -362,7 +359,8 @@
     dma = pltpu.SemaphoreType.DMA((n,))
     return pl.pallas_call(
         functools.partial(fused_kernel, n, unit_rows),
-        in_specs=[pl.BlockSpec(memory_space=pltpu.SMEM)] + [vmem] * 4,
+        in_specs=[pl.BlockSpec(memory_space=pltpu.SMEM), pl.BlockSpec(memory_space=pl.ANY)]
+        + [vmem] * 3,
         out_specs=[vmem] * 3,
         out_shape=[
             jax.ShapeDtypeStruct((rows, n * slab), BF16),
@@ -370,6 +368,7 @@
             jax.ShapeDtypeStruct((rank, out_width), F32),
         ],
         scratch_shapes=[
+            pltpu.VMEM((tokens, slab), BF16),
             pltpu.VMEM((n, unit_rows, SLOTS * rank), BF16),
             pltpu.VMEM((n, unit_rows, SLOTS * rank), BF16),
             pltpu.VMEM((unit_rows, SLOTS * rank), BF16),
@@ -379,12 +378,12 @@
             pltpu.VMEM((tokens, n * rank), BF16),
             pltpu.VMEM((n, rank, slab), BF16),
             pltpu.VMEM((n, rank, slab), BF16),
-        ] + [dma] * 8,
+        ] + [dma] * 10 + [pltpu.SemaphoreType.DMA((1,))],
         compiler_params=pltpu.CompilerParams(
             collective_id=0, has_side_effects=True, vmem_limit_bytes=52 * 2**20),
         cost_estimate=pl.CostEstimate(
             flops=2 * tokens * slab * out_width * 4, bytes_accessed=30 * 2**20, transcendentals=0),
-    )(unit_place, acts_slab, both_all, weight, down_slabs)
+    )(unit_place, acts, both_all, weight, down_slabs)
 
 
 def shards(
@@ -419,9 +418,9 @@
     adapters = n * up_t.shape[0]
     if tokens * out_width <= 4 * 2**20 and slab % BLK == 0 and adapters == n and n % PLANE == 0:
         both = jnp.concatenate([output_gradient, up_t[0]], axis=0)
-        acts_slab, down_slabs, both_all = exchange(n, acts, down_t[0], both)
+        down_slabs, both_all = exchange(n, down_t[0], both)
         input_gradient, down_out, up_out = fused(
-            n, unit_place, acts_slab, both_all, weight, down_slabs)
+            n, unit_place, acts, both_all, weight, down_slabs)
         return (
             input_gradient,
             down_out[None].transpose(0, 2, 1),

time: 263 us -> 266 us (1.011)
  Pallas kernels: 250 us -> 253 us
    pallas_call x1, Pallas kernels: 117 us -> 177 us  [fused(): pl.pallas_call(functools.partial(fused_kernel, n, unit_rows), in_specs=[p...]
    pallas_call x1, Pallas kernels: 133 us -> 76.2 us  [exchange(): pl.pallas_call(functools.partial(exchange_kernel, n), in_specs=[anywhere]...]
where the time goes in v4:
time: 266 us; the launch traced here: 265 us
  Pallas kernels  253 us (95%)
  local copies, waits for them, and re-layouts  8.21 us (3%)
  other arithmetic  3.09 us (1%)
    pallas_call x1, Pallas kernels, fused(): pl.pallas_call(functools.partial(fused_kernel, n, unit_rows), in_specs=[p...  177 us
    pallas_call x1, Pallas kernels, exchange(): pl.pallas_call(functools.partial(exchange_kernel, n), in_specs=[anywhere]...  76.2 us
    unnamed x13, local copies, waits for them, and re-layouts  6.5 us

profile of v4, /device:TPU:13, one launch (start us, length us, event | category | flops | bytes accessed | tf_op | source)
XLA Modules:
  0.0 265.5 jit_solution(9513155961711327394)
XLA Ops:
  0.6 0.0 copy-start.3
  0.6 0.0 copy-start.2
  0.7 0.8 reduce
  1.5 0.1 reshape.75
  1.6 0.1 copy.17
  1.6 0.7 select_reduce_fusion.place
  2.4 0.8 copy.16
  3.2 1.0 gather_fusion
  4.2 0.0 copy-done.3
  4.2 0.0 copy-done.2
  4.2 0.0 copy-start.1
  4.2 0.8 pad_maximum_fusion.both
  5.0 0.6 mul.15
  5.6 0.0 copy-done.1
  5.6 0.7 fusion.weight
  6.4 76.2 %shard_map.103 = (bf16[16,64,512]{2,1,0:T(8,128)(2,1)}, bf16[16,224,1024]{2,1,0:T(8,128)(2,1)}) custom-call(bf16[64,8192]{1,0:T(8,128)(2,1)} %bitcast.23, bf16[224,1024]{1,0:T(8,128)(2,1)} %pad_maximum_fusion.both), custom_call_target="tpu_custom_call" | custom-call | bytes 209715200 | tf_op jit(solution)/shard_map/pallas_call | solution.py:162
  82.5 177.3 %shard_map.104 = (bf16[160,8192]{1,0:T(8,128)(2,1)}, f32[64,8192]{1,0:T(8,128)}, f32[64,1024]{1,0:T(8,128)S(1)}) custom-call(s32[32]{0:T(128)S(1)} %select_reduce_fusion.place, bf16[160,8192]{1,0:T(8,128)(2,1)} %acts_own.1, bf16[16,224,1024]{2,1,0:T(8,128)(2,1)} %get-tuple-element.8.both_all, bf16[512,1024]{1,0:T(8,128)(2,1)S(1)} %fusion.weight, ...), custom_call_target="tpu_custom_call" | custom-call | flops 10737418240 | bytes 31457280 | tf_op jit(solution)/shard_map/pallas_call | solution.py:360
  259.8 0.0 copy-start
  259.8 3.6 %copy.23 = bf16[160,8192]{1,0:T(8,128)(2,1)} copy(bf16[160,8192]{1,0:T(8,128)(2,1)} %get-tuple-element.16) | data formatting | bytes 5242880
  263.4 0.0 copy-done
  263.5 1.3 copy.24
  264.8 0.7 copy.25
  (2 shorter events, 0.0 us)
Async XLA Ops:
  0.6 3.6 %copy-start.3 = (bf16[1,1024,64]{1,2,0:T(8,128)(2,1)S(1)}, bf16[1,1024,64]{1,2,0:T(8,128)(2,1)}, u32[]{:S(2)}) copy-start(bf16[1,1024,64]{1,2,0:T(8,128)(2,1)} %param.13) | copy-start | bytes 393220
  0.6 3.6 %copy-start.2 = (bf16[160,1024]{1,0:T(8,128)(2,1)S(1)}, bf16[160,1024]{1,0:T(8,128)(2,1)}, u32[]{:S(2)}) copy-start(bf16[160,1024]{1,0:T(8,128)(2,1)} %param.9) | copy-start | bytes 983044
  4.2 1.4 copy-start.1
  259.8 3.6 %copy-start = (f32[64,8192]{1,0:T(8,128)S(1)}, f32[64,8192]{1,0:T(8,128)}, u32[]{:S(2)}) copy-start(f32[64,8192]{1,0:T(8,128)} %get-tuple-element.11) | copy-start | bytes 6291460
